TPU v7x, 256 devices: a whole 4x4x8 slice. The times are simulated.
256 devices in a mesh: row: 8 (over z_lo, y), col: 32 (over z_hi, x, core).
Axes of the slice: x: 4, y: 4, z: 8 (z_hi: 4, z_lo: 2; z = z_hi * 2 + z_lo), core: 2. Of those that a mesh axis runs over, the one named last changes fastest.
Arguments:
- stream: bfloat16 [1024, 8192], P('row', 'col'), may hold values from -36 to 36
- heads_out: bfloat16 [1024, 8192], P('row', 'col'), may hold values from -6 to 6
- w_out: bfloat16 [8192, 8192], P('row', 'col'), may hold values from -0.0625 to 0.0625
- norm_gain: float32 [8192], replicated, may hold values from 0.1 to 1.9
- expert_ids: int32 [1024, 2], P('row'), may hold values from 0 to 15, all different within a row; in each aligned block of 128 rows (0 to 127, 128 to 255, ...) at most 32 rows name the same one
- route_gates: float32 [1024, 2], P('row'), may hold values from 0.2 to 1
- w_gate: bfloat16 [8192, 65536], P(None, ('row', 'col')), may hold values from -0.0625 to 0.0625
- w_up: bfloat16 [8192, 65536], P(None, ('row', 'col')), may hold values from -0.0625 to 0.0625
- w_down: bfloat16 [65536, 8192], P(('row', 'col')), may hold values from -0.09375 to 0.09375
Outputs:
- mixed: bfloat16 [1024, 8192], P('row', 'col')
Inputs may be any that keep to these rules, and one draw needn't show every extreme that they name: `expert_ids`: each row names two different experts. Within the 128 rows of one index of row no expert is named more than 32 times, and in some such block an expert is named exactly 32 times.
All inputs are finite; a program needn't handle non-finite values.
Results may differ from a plain program's by a relative error of at most 0.011.
Values may be sent and summed in bfloat16 or wider, within the bound.
A program may use at most 128 MiB of HBM per device.

v0:
```python
import jax
import jax.numpy as jnp
from jax import lax
from jax.sharding import PartitionSpec as P


def normalize(values, gain):
    wide = values.astype(jnp.float32)
    square = jnp.mean(wide * wide, axis=-1, keepdims=True)
    return (wide * lax.rsqrt(square + 1e-05) * gain).astype(jnp.bfloat16)


def slot_positions(expert_ids, block_rows, expert_count):
    one_hot = (expert_ids[:, :, None] == jnp.arange(expert_count, dtype=jnp.int32)).astype(
        jnp.int32
    )
    grouped = one_hot.reshape(-1, block_rows * 2, expert_count)
    earlier = jnp.cumsum(grouped, axis=1) - grouped
    return jnp.sum(earlier * grouped, axis=-1).reshape(expert_ids.shape)


def per_device(stream, heads_out, w_out, norm_gain, expert_ids, route_gates, w_gate, w_up, w_down):
    token_count = stream.shape[0]
    feature_count = stream.shape[1]
    full_width = w_gate.shape[0]
    row_count = lax.axis_size("row")
    expert_count = 2 * row_count
    capacity = min(token_count, 4 * token_count // expert_count)
    local_expert = lax.axis_index("col") // (lax.axis_size("col") // 2)
    heads_whole = lax.all_gather(heads_out, "col", axis=1, tiled=True)
    projected = jnp.dot(
        heads_whole,
        lax.all_gather(w_out, "row", axis=0, tiled=True),
        preferred_element_type=jnp.float32,
    )
    residual = (stream.astype(jnp.float32) + projected).astype(jnp.bfloat16)
    position = slot_positions(expert_ids, token_count, expert_count)
    slot_index = expert_ids * capacity + position
    slot_range = jnp.arange(expert_count * capacity, dtype=jnp.int32)
    matches = jnp.sum((slot_index[:, :, None] == slot_range).astype(jnp.int32), axis=1)
    token_of_slot = jnp.sum(matches * jnp.arange(token_count, dtype=jnp.int32)[:, None], axis=0)
    filled = jnp.sum(matches, axis=0).astype(jnp.bfloat16)
    whole = lax.all_gather(residual, "col", axis=1, tiled=True)
    source = normalize(whole, norm_gain)
    payload = (jnp.take(source, token_of_slot, axis=0) * filled[:, None]).reshape(
        expert_count, capacity, source.shape[1]
    )
    arrived = lax.all_to_all(payload, "row", split_axis=0, concat_axis=0, tiled=True)
    grouped = arrived.reshape(row_count, 2, capacity, full_width)
    slot_rows = lax.dynamic_index_in_dim(grouped, local_expert, 1, keepdims=False).reshape(
        -1, full_width
    )
    gate_pre = jnp.dot(slot_rows, w_gate, preferred_element_type=jnp.float32)
    up_pre = jnp.dot(slot_rows, w_up, preferred_element_type=jnp.float32)
    activated = (jax.nn.silu(gate_pre) * up_pre).astype(jnp.bfloat16)
    partial_value = jnp.dot(activated, w_down, preferred_element_type=jnp.float32)
    which = (jnp.arange(2, dtype=jnp.int32) == local_expert).astype(jnp.float32)
    placed = partial_value.reshape(row_count, 1, capacity, full_width) * which[None, :, None, None]
    summed = lax.psum_scatter(placed.astype(jnp.bfloat16), "col", scatter_dimension=3, tiled=True)
    returned = lax.all_to_all(summed, "row", split_axis=0, concat_axis=0, tiled=True)
    returned = returned.reshape(expert_count * capacity, feature_count)
    picked = (
        jnp.take(returned, slot_index.reshape(-1), axis=0)
        .reshape(token_count, 2, feature_count)
        .astype(jnp.float32)
    )
    mixed = residual.astype(jnp.float32) + jnp.sum(route_gates[:, :, None] * picked, axis=1)
    return mixed.astype(jnp.bfloat16)


def solution(mesh):
    return jax.shard_map(
        per_device,
        mesh=mesh,
        in_specs=(
            P("row", "col"),
            P("row", "col"),
            P("row", "col"),
            P(),
            P("row", None),
            P("row", None),
            P(None, ("row", "col")),
            P(None, ("row", "col")),
            P(("row", "col"), None),
        ),
        out_specs=P("row", "col"),
        check_vma=False,
    )
```

profile of v0, /device:TPU:1, one launch (start us, length us, event | category | flops | bytes accessed | tf_op | source)
XLA Modules:
  0.0 464.0 jit_solution(7326693740459309367)
XLA Ops:
  6.5 0.7 all-gather.4.cloned.1.call-update
  7.3 0.7 all-gather.6.cloned.1.call-update
  8.1 61.9 %all-gather.4.cloned.1.call-done = bf16[128,8192]{1,0:T(8,128)(2,1)} async-done(((bf16[128,256]{1,0:T(8,128)(2,1)}), bf16[128,8192]{1,0:T(8,128)(2,1)}) %all-gather.4.cloned.1.call-update) | async-done | bytes 2097168 | tf_op jit(solution)/shard_map/all_gather | solution.py:30
  70.0 54.0 %all-gather.6.cloned.1.call-done = bf16[8192,256]{1,0:T(8,128)(2,1)} async-done(((bf16[1024,256]{1,0:T(8,128)(2,1)}), bf16[8192,256]{1,0:T(8,128)(2,1)}) %all-gather.6.cloned.1.call-update) | async-done | bytes 4194320 | tf_op jit(solution)/shard_map/all_gather | solution.py:33
  124.0 4.2 fusion.5
  128.4 0.1 eq.48
  128.6 0.6 reduce-window.6
  129.2 0.2 slice_reduce_fusion
  129.6 0.1 reshape.206
  129.9 0.1 convert_reduce_fusion
  130.3 53.2 %all-gather.8.cloned.1.call-done = bf16[128,8192]{1,0:T(8,128)(2,1)} async-done(((bf16[128,256]{1,0:T(8,128)(2,1)}), bf16[128,8192]{1,0:T(8,128)(2,1)}) %all-gather.8.cloned.1.call-update) | async-done | bytes 2097168 | tf_op jit(solution)/shard_map/all_gather | solution.py:43
  183.5 2.1 fusion
  185.6 2.2 fusion.2
  187.8 7.8 %gather_fusion = bf16[512,8192]{1,0:T(8,128)(2,1)} fusion(bf16[128,8192]{1,0:T(8,128)(2,1)S(1)} %fusion.2, s32[1024]{0:T(1024)S(1)} %pad_clamp_fusion.1), kind=kCustom, calls=%fused_computation | custom fusion | bytes 16779264 | tf_op jit(solution)/shard_map/jit(_take)/gather | solution.py:45
  195.6 7.5 %select_multiply_fusion = bf16[16,32,8192]{2,1,0:T(8,128)(2,1)} fusion(bf16[16,32,8192]{2,1,0:T(8,128)(2,1)} %bitcast.30, pred[16,32]{1,0:T(8,128)(4,1)S(1)} %compare_and_fusion, bf16[16,32]{1,0:T(8,128)(2,1)S(1)} %convert_element_type.65), kind=kLoop, calls=%fused_computation.3 | loop fusion | flops 8388608 | bytes 16778752 | tf_op jit(solution)/shard_map/mul | solution.py:45
  203.1 5.0 %all-to-all-start = ((bf16[16,32,8192]{2,1,0:T(8,128)(2,1)}), bf16[16,32,8192]{2,1,0:T(8,128)(2,1)}, u32[]{:S(2)}, u32[]{:S(2)}) async-start(bf16[16,32,8192]{2,1,0:T(8,128)(2,1)} %select_multiply_fusion), calls=%async_computation | async-start | bytes 16777216 | tf_op jit(solution)/shard_map/all_to_all | solution.py:48
  208.1 0.2 reduce-scatter.2.cloned.1.call-start
  208.4 93.4 %all-to-all-done = bf16[16,32,8192]{2,1,0:T(8,128)(2,1)} async-done(((bf16[16,32,8192]{2,1,0:T(8,128)(2,1)}), bf16[16,32,8192]{2,1,0:T(8,128)(2,1)}, u32[]{:S(2)}, u32[]{:S(2)}) %all-to-all-start) | async-done | bytes 8388640 | tf_op jit(solution)/shard_map/all_to_all | solution.py:48
  301.8 2.6 constant_dynamic-slice_fusion
  304.4 2.0 copy-done
  306.4 1.2 fusion.14
  307.6 12.4 %fusion.4 = f32[256,8192]{1,0:T(8,128)} fusion(bf16[256,8192]{1,0:T(8,128)(2,1)} %param.17, bf16[256,8192]{1,0:T(8,128)(2,1)} %bitcast.32, bf16[8192,256]{1,0:T(8,128)(2,1)} %param.16, f32[256,256]{1,0:T(8,128)S(1)} %fusion.14), kind=kOutput, calls=%fused_computation.11 | convolution fusion | flops 2147876864 | bytes 21233664 | tf_op jit(solution)/shard_map/dot_general | solution.py:56
  320.0 8.2 %multiply_convert_fusion = bf16[8,2,32,8192]{3,2,1,0:T(8,128)(2,1)} fusion(f32[2]{0:T(128)S(1)} %compare_convert_fusion.1, f32[8,32,8192]{2,1,0:T(8,128)} %bitcast.29), kind=kLoop, calls=%fused_computation.2 | loop fusion | flops 8388608 | bytes 16777224 | tf_op jit(solution)/shard_map/convert_element_type | solution.py:59
  328.3 116.6 %reduce-scatter.2.cloned.1.call-done = bf16[8,2,32,256]{3,2,1,0:T(8,128)(2,1)} async-done(((bf16[8,2,32,8192]{3,2,1,0:T(8,128)(2,1)}), bf16[8,2,32,256]{3,2,1,0:T(8,128)(2,1)}) %reduce-scatter.2.cloned.1.call-update) | async-done | bytes 262160 | tf_op jit(solution)/shard_map/reduce_scatter | solution.py:59
  444.8 4.2 all-to-all-start.1
  449.1 0.1 reshape.210
  449.3 0.1 copy.34
  449.4 0.1 copy.28
  449.5 5.5 %all-to-all-done.1 = bf16[8,2,32,256]{3,2,1,0:T(8,128)(2,1)S(1)} async-done(((bf16[8,2,32,256]{3,2,1,0:T(8,128)(2,1)}), bf16[8,2,32,256]{3,2,1,0:T(8,128)(2,1)S(1)}, u32[]{:S(2)}, u32[]{:S(2)}) %all-to-all-start.1) | async-done | bytes 262176 | tf_op jit(solution)/shard_map/all_to_all | solution.py:60
  455.1 1.2 gather_fusion.1
  456.3 0.5 multiply_reduce_fusion
  456.8 0.6 add_convert_fusion
  (40 shorter events, 1.1 us)
Async XLA Ops:
  6.5 121.8 %copy-start.3 = (s32[128,2]{0,1:T(2,128)S(1)}, s32[128,2]{0,1:T(2,128)}, u32[]{:S(2)}) copy-start(s32[128,2]{0,1:T(2,128)} %param.13) | copy-start | bytes 3076
  6.5 63.5 %all-gather.4.cloned.1.call-start = ((), (), s32[]{:S(2)}) async-start(), calls=%async_computation.3 | async-start | bytes 2162688 | tf_op jit(solution)/shard_map/all_gather | solution.py:30
  7.3 116.8 %all-gather.6.cloned.1.call-start = ((), (), s32[]{:S(2)}) async-start(), calls=%async_computation.4 | async-start | bytes 4718592 | tf_op jit(solution)/shard_map/all_gather | solution.py:33
  8.0 177.6 %copy-start.2 = (f32[8192]{0:T(1024)S(1)}, f32[8192]{0:T(1024)}, u32[]{:S(2)}) copy-start(f32[8192]{0:T(1024)} %param.12) | copy-start | bytes 98308
  8.0 175.5 %all-gather.8.cloned.1.call-start = ((), (), s32[]{:S(2)}) async-start(), calls=%async_computation.5 | async-start | bytes 2162688 | tf_op jit(solution)/shard_map/all_gather | solution.py:43
  203.1 98.7 %all-to-all-start = ((bf16[16,32,8192]{2,1,0:T(8,128)(2,1)}), bf16[16,32,8192]{2,1,0:T(8,128)(2,1)}, u32[]{:S(2)}, u32[]{:S(2)}) async-start(bf16[16,32,8192]{2,1,0:T(8,128)(2,1)} %select_multiply_fusion), calls=%async_computation | async-start | bytes 16777216 | tf_op jit(solution)/shard_map/all_to_all | solution.py:48
  208.1 236.7 %reduce-scatter.2.cloned.1.call-start = ((), (), s32[]{:S(2)}) async-start(), calls=%async_computation.6 | async-start | bytes 8650752 | tf_op jit(solution)/shard_map/reduce_scatter | solution.py:59
  301.8 4.6 copy-start.5
  304.4 2.0 copy-start
  328.2 121.2 %copy-start.4 = (f32[128,2]{0,1:T(2,128)S(1)}, f32[128,2]{0,1:T(2,128)}, u32[]{:S(2)}) copy-start(f32[128,2]{0,1:T(2,128)} %param.14) | copy-start | bytes 3076
  328.2 128.6 %copy-start.1 = (bf16[128,256]{1,0:T(8,128)(2,1)S(1)}, bf16[128,256]{1,0:T(8,128)(2,1)}, u32[]{:S(2)}) copy-start(bf16[128,256]{1,0:T(8,128)(2,1)} %fusion.5) | copy-start | bytes 196612
  444.8 10.2 %all-to-all-start.1 = ((bf16[8,2,32,256]{3,2,1,0:T(8,128)(2,1)}), bf16[8,2,32,256]{3,2,1,0:T(8,128)(2,1)S(1)}, u32[]{:S(2)}, u32[]{:S(2)}) async-start(bf16[8,2,32,256]{3,2,1,0:T(8,128)(2,1)} %reduce-scatter.2.cloned.1.call-done), calls=%async_computation.2 | async-start | bytes 524288 | tf_op jit(solution)/shard_map/all_to_all | solution.py:60
Sparse Core Ops, SparseCore 0:
  9.8 60.1 all-gather.3
  71.8 52.2 all-gather.5
  128.4 55.0 all-gather.7
  328.4 116.4 reduce-scatter.1
where the time goes:
time: 465 us; the launch traced here: 464 us
  waiting for transfers between devices  386 us (83%)
  other arithmetic  22 us (5%)
  matrix products  17.9 us (4%)
  local copies, waits for them, and re-layouts  15.1 us (3%)
  between operations  13.3 us (3%)
  starting transfers between devices  9.5 us (2%)
    reduce_scatter x1, waiting for transfers between devices, per_device(): lax.psum_scatter(placed.astype(jnp.bfloat16), 'col', scatter_dimension=3,...  117 us
    all_to_all x1, waiting for transfers between devices, per_device(): lax.all_to_all(payload, 'row', split_axis=0, concat_axis=0, tiled=True)  93.4 us
    all_gather x1, waiting for transfers between devices, per_device(): heads_whole = lax.all_gather(heads_out, 'col', axis=1, tiled=True)  61.9 us
    all_gather x1, waiting for transfers between devices, per_device(): lax.all_gather(w_out, 'row', axis=0, tiled=True)  54 us
    all_gather x1, waiting for transfers between devices, per_device(): whole = lax.all_gather(residual, 'col', axis=1, tiled=True)  53.2 us
    dot_general x1, matrix products, per_device(): jnp.dot(activated, w_down, preferred_element_type=jnp.float32)  12.4 us
  transfers between devices with their start and end apart: 6, of which 6 were waited for; matrix products, arithmetic and copies ran while one was open for 1% of the time, Pallas kernels for 0%

commit v1 on v0

v1 whole, which is shorter than its diff:
```python
import jax
import jax.numpy as jnp
from jax import lax
from jax.experimental import pallas as pl
from jax.experimental.pallas import tpu as pltpu
from jax.sharding import PartitionSpec as P

MESH = pl.DeviceIdType.MESH
BF = jnp.bfloat16
F32 = jnp.float32
WIDTH = 8192
CHUNK_ORDER_IN = (0, 1, 3, 2)
CHUNK_ORDER_OUT = (2, 1, 3, 0)


def place(z_lo, y, z_hi, x, core):
    return (z_lo * 4 + y, z_hi * 8 + x * 2 + core)


def local_copy(src, dst, sem):
    copy = pltpu.make_async_copy(src, dst, sem)
    copy.start()


def send(src, dst, send_sem, recv_sem, device):
    copy = pltpu.make_async_remote_copy(
        src_ref=src,
        dst_ref=dst,
        send_sem=send_sem,
        recv_sem=recv_sem,
        device_id=device,
        device_id_type=MESH,
    )
    copy.start()


def wait_bytes(view, sem):
    pltpu.make_async_copy(view, view, sem).wait()


def dot(a, b):
    return jnp.dot(a, b, preferred_element_type=F32)


def kernel(
    stream, heads, w_out, gain, ids, gates, w_gate, w_up, w_down,
    out,
    heads_in, w_out_pair, proj_out, proj_in, stream_v, gate_w, up_w, down_w,
    payload, tokens, pre, pre_in, squares, squares_in, act,
    far_out, right_out, left_out, far_left, far_right, from_left, from_right, summed, final_in,
    in_sem, w_sem, wr_sem, ws_sem,
    p1_recv, p1_send, px_recv, px_send, rs_recv, rs_send,
    d1_recv, d1_send, d2_recv, d2_send, d3_recv, d3_send, ex_recv, ex_send,
    f_recv, f_send, g_recv, g_send, z_recv, z_send,
):
    row = lax.axis_index("row")
    col = lax.axis_index("col")
    z_lo, y = lax.div(row, 4), lax.rem(row, 4)
    z_hi = lax.div(col, 8)
    x = lax.rem(lax.div(col, 2), 4)
    core = lax.rem(col, 2)
    other = 1 - core
    right = lax.rem(x + 1, 4)
    left = lax.rem(x + 3, 4)
    far = lax.rem(x + 2, 4)
    right_dev = place(z_lo, y, z_hi, right, core)
    left_dev = place(z_lo, y, z_hi, left, core)
    pair_dev = place(z_lo, y, z_hi, x, other)

    own_group = lax.rem(x, 2) * 2 + core
    p_row_lo = lax.div(z_hi, 2)
    p_row_y = lax.rem(z_hi, 2) * 2 + lax.div(x, 2)
    p_self = jnp.logical_and(jnp.logical_and(p_row_lo == z_lo, p_row_y == y), z_lo == core)
    for dz in (2, 1, 3, 0):
        for dx in (2, 1, 3, 0):
            to_x = lax.rem(x + dx, 4)
            to_z = lax.rem(z_hi + dz, 4)
            src = heads.at[pl.ds(to_x * 32, 32), :]
            dst = heads_in.at[to_x, own_group, y]
            device = place(p_row_lo, p_row_y, to_z, to_x, z_lo)
            if dz == 0 and dx == 0:
                @pl.when(p_self)
                def _():
                    local_copy(src, dst, p1_recv)

                @pl.when(jnp.logical_not(p_self))
                def _():
                    send(src, dst, p1_send.at[1], p1_recv, device)
            else:
                send(src, dst, p1_send.at[0], p1_recv, device)

    local_copy(w_out, w_out_pair.at[core], w_sem.at[0])
    send(w_out, w_out_pair.at[core], ws_sem.at[0], wr_sem.at[0], pair_dev)
    local_copy(stream, stream_v, in_sem.at[0])
    local_copy(w_gate.at[:, core], gate_w.at[core], w_sem.at[1])
    local_copy(w_up.at[:, core], up_w.at[core], w_sem.at[2])
    send(w_gate.at[:, other], gate_w.at[core], ws_sem.at[1], wr_sem.at[1], pair_dev)
    send(w_up.at[:, other], up_w.at[core], ws_sem.at[2], wr_sem.at[2], pair_dev)

    def load_down(b, carry):
        mine = pl.multiple_of((2 * b + core) * 256, 256)
        theirs = pl.multiple_of((2 * b + other) * 256, 256)
        local_copy(w_down.at[:, pl.ds(mine, 256)], down_w.at[core, b], w_sem.at[3])
        send(w_down.at[:, pl.ds(theirs, 256)], down_w.at[core, b], ws_sem.at[3], wr_sem.at[3], pair_dev)
        return carry

    lax.fori_loop(0, 16, load_down, 0)

    lane = lax.broadcasted_iota(jnp.int32, (128, 128), 1)
    sub = lax.broadcasted_iota(jnp.int32, (128, 128), 0)
    first = (ids[:, 0:1] == lane).astype(F32)
    second = (ids[:, 1:2] == lane).astype(F32)
    earlier = dot((lane < sub).astype(BF), (first + second).astype(BF))
    slot_lane = lax.broadcasted_iota(jnp.int32, (128, 512), 1)
    slot0 = ids[:, 0:1] * 32 + jnp.sum(earlier * first, axis=1, keepdims=True).astype(jnp.int32)
    slot1 = ids[:, 1:2] * 32 + jnp.sum(earlier * second, axis=1, keepdims=True).astype(jnp.int32)
    pick0 = (slot0 == slot_lane).astype(F32)
    pick1 = (slot1 == slot_lane).astype(F32)
    spread = (pick0 + pick1).T.astype(BF)
    pre[...] = jnp.zeros_like(pre)
    squares[...] = jnp.zeros_like(squares)

    def project(group):
        rows = [heads_in[group, j].reshape(128, 256) for j in range(4)]
        for dc in range(2):
            c = core if dc == 0 else other
            total = dot(rows[0], w_out_pair[c, 0:256, :])
            for j in range(1, 4):
                total = total + dot(rows[j], w_out_pair[c, j * 256:(j + 1) * 256, :])
            proj_out[group, c] = total.astype(BF).reshape(4, 32, 256)
        for dy in (2, 1, 3, 0):
            to_y = lax.rem(y + dy, 4)
            for dc in range(2):
                c = core if dc == 0 else other
                src = proj_out.at[group, c, to_y]
                dst = proj_in.at[row, pl.ds(group * 32, 32), :]
                device = place(core, to_y, z_hi, x, c)
                if dy == 0 and dc == 0:
                    @pl.when(z_lo == core)
                    def _():
                        local_copy(src, dst, rs_recv)

                    @pl.when(z_lo != core)
                    def _():
                        send(src, dst, rs_send.at[1], rs_recv, device)
                else:
                    send(src, dst, rs_send.at[0], rs_recv, device)

    wait_bytes(heads_in.at[x], p1_recv)
    send(heads_in.at[x], heads_in.at[x], px_send.at[0], px_recv.at[0], right_dev)
    send(heads_in.at[x], heads_in.at[x], px_send.at[1], px_recv.at[1], left_dev)
    wait_bytes(w_out_pair.at[core], w_sem.at[0])
    wait_bytes(w_out_pair.at[other], wr_sem.at[0])
    project(x)
    wait_bytes(heads_in.at[left], px_recv.at[0])
    send(heads_in.at[left, 0:2], heads_in.at[left, 0:2], px_send.at[2], px_recv.at[2], right_dev)
    wait_bytes(heads_in.at[right], px_recv.at[1])
    send(heads_in.at[right, 2:4], heads_in.at[right, 2:4], px_send.at[3], px_recv.at[3], left_dev)
    project(left)
    project(right)
    wait_bytes(heads_in.at[far, 0:2], px_recv.at[2])
    wait_bytes(heads_in.at[far, 2:4], px_recv.at[3])
    project(far)

    wait_bytes(stream_v, in_sem.at[0])
    wait_bytes(proj_in, rs_recv)
    residual = stream_v[...].astype(F32)
    for r in range(8):
        residual = residual + proj_in[r].astype(F32)
    stream_v[...] = residual.astype(BF)

    payload[...] = dot(spread, stream_v[...]).astype(BF).reshape(16, 32, 256)
    for dz in CHUNK_ORDER_IN:
        to_z = lax.rem(z_hi + dz, 4)
        for dl in (1, 0):
            to_lo = z_lo if dl == 0 else 1 - z_lo
            for dy in (2, 1, 3, 0):
                to_y = lax.rem(y + dy, 4)
                expert = 2 * (to_lo * 4 + to_y) + lax.div(to_z, 2)
                src = payload.at[expert]
                dst = tokens.at[x, z_hi, row]
                if dz == 0 and dl == 0 and dy == 0:
                    local_copy(src, dst, d1_recv.at[dz])
                else:
                    send(src, dst, d1_send.at[dz], d1_recv.at[dz], place(to_lo, to_y, to_z, x, core))

    wait_bytes(gate_w.at[core], w_sem.at[1])
    wait_bytes(up_w.at[core], w_sem.at[2])
    wait_bytes(gate_w.at[other], wr_sem.at[1])
    wait_bytes(up_w.at[other], wr_sem.at[2])

    def absorb(from_x, from_z):
        block = tokens[from_x, from_z].reshape(256, 256).astype(F32)
        square = block * block
        squares[...] += square[:, 0:128] + square[:, 128:256]
        scaled = (block * gain[from_z * 8 + from_x * 2 + core]).astype(BF)
        b = from_z * 4 + from_x
        for c in range(2):
            pre[c] += dot(scaled, gate_w[c, b])
            pre[2 + c] += dot(scaled, up_w[c, b])

    def chunk_z(i):
        return lax.rem(z_hi + 4 - CHUNK_ORDER_IN[i], 4)

    def gather_first(i):
        zc = chunk_z(i)
        wait_bytes(tokens.at[x, zc], d1_recv.at[CHUNK_ORDER_IN[i]])
        view = tokens.at[x, zc]
        send(view, view, d2_send.at[0, i], d2_recv.at[0, i], right_dev)
        send(view, view, d2_send.at[1, i], d2_recv.at[1, i], left_dev)
        absorb(x, zc)

    def gather_second(i):
        zc = chunk_z(i)
        wait_bytes(tokens.at[left, zc], d2_recv.at[0, i])
        view = tokens.at[left, zc, 0:4]
        send(view, view, d3_send.at[0, i], d3_recv.at[0, i], right_dev)
        wait_bytes(tokens.at[right, zc], d2_recv.at[1, i])
        view = tokens.at[right, zc, 4:8]
        send(view, view, d3_send.at[1, i], d3_recv.at[1, i], left_dev)
        absorb(left, zc)
        absorb(right, zc)

    def gather_third(i):
        zc = chunk_z(i)
        wait_bytes(tokens.at[far, zc, 0:4], d3_recv.at[0, i])
        wait_bytes(tokens.at[far, zc, 4:8], d3_recv.at[1, i])
        absorb(far, zc)

    for i in range(6):
        if i < 4:
            gather_first(i)
        if 1 <= i < 5:
            gather_second(i - 1)
        if i >= 2:
            gather_third(i - 2)

    send(pre, pre_in, ex_send.at[0], ex_recv.at[0], pair_dev)
    send(squares, squares_in, ex_send.at[1], ex_recv.at[1], pair_dev)
    wait_bytes(squares_in, ex_recv.at[1])
    wait_bytes(pre_in, ex_recv.at[0])
    mean = jnp.sum(squares[...] + squares_in[...], axis=1, keepdims=True) / WIDTH
    scale = lax.rsqrt(mean + 1e-05)
    for c in range(2):
        gate_pre = (pre[c] + pre_in[c]) * scale
        up_pre = (pre[2 + c] + pre_in[2 + c]) * scale
        act[c] = (gate_pre / (1.0 + jnp.exp(-gate_pre)) * up_pre).astype(BF)

    wait_bytes(down_w.at[core], w_sem.at[3])
    wait_bytes(down_w.at[other], wr_sem.at[3])

    def down(start, rows, to_x, zc):
        b = zc * 4 + to_x
        return dot(act[0, start:start + rows, :], down_w[0, b]) + dot(
            act[1, start:start + rows, :], down_w[1, b]
        )

    def out_z(i):
        return lax.rem(z_hi + CHUNK_ORDER_OUT[i], 4)

    def return_first(i):
        zc = out_z(i)
        far_out[i] = down(0, 256, far, zc).astype(BF)
        send(far_out.at[i, 0:128], far_left.at[i], f_send.at[0, i], f_recv.at[0, i], right_dev)
        send(far_out.at[i, 128:256], far_right.at[i], f_send.at[1, i], f_recv.at[1, i], left_dev)
        right_out[i, 128:256] = down(128, 128, right, zc).astype(BF)
        send(right_out.at[i, 128:256], from_left.at[i, 128:256], g_send.at[0, i], g_recv.at[0, i], right_dev)
        left_out[i, 0:128] = down(0, 128, left, zc).astype(BF)
        send(left_out.at[i, 0:128], from_right.at[i, 0:128], g_send.at[1, i], g_recv.at[1, i], left_dev)

    def return_second(i):
        zc = out_z(i)
        mine = down(0, 128, right, zc)
        wait_bytes(far_left.at[i], f_recv.at[0, i])
        right_out[i, 0:128] = (mine + far_left[i].astype(F32)).astype(BF)
        send(right_out.at[i, 0:128], from_left.at[i, 0:128], g_send.at[0, i], g_recv.at[0, i], right_dev)
        mine = down(128, 128, left, zc)
        wait_bytes(far_right.at[i], f_recv.at[1, i])
        left_out[i, 128:256] = (mine + far_right[i].astype(F32)).astype(BF)
        send(left_out.at[i, 128:256], from_right.at[i, 128:256], g_send.at[1, i], g_recv.at[1, i], left_dev)

    def return_third(i):
        zc = out_z(i)
        mine = down(0, 256, x, zc)
        wait_bytes(from_left.at[i], g_recv.at[0, i])
        wait_bytes(from_right.at[i], g_recv.at[1, i])
        total = mine + from_left[i].astype(F32) + from_right[i].astype(F32)
        summed[i] = total.astype(BF).reshape(8, 32, 256)
        for dl in (1, 0):
            to_lo = z_lo if dl == 0 else 1 - z_lo
            for dy in (2, 1, 3, 0):
                to_y = lax.rem(y + dy, 4)
                src = summed.at[i, to_lo * 4 + to_y]
                dst = final_in.at[row, z_hi]
                if CHUNK_ORDER_OUT[i] == 0 and dl == 0 and dy == 0:
                    local_copy(src, dst, z_recv)
                else:
                    send(src, dst, z_send.at[i], z_recv, place(to_lo, to_y, zc, x, core))

    return_first(0)
    return_first(1)
    return_second(0)
    return_first(2)
    return_second(1)
    return_third(0)
    return_first(3)
    return_second(2)
    return_third(1)
    return_second(3)
    return_third(2)
    return_third(3)

    wait_bytes(final_in, z_recv)
    pieces = final_in[...].astype(F32).reshape(16, 2, 32, 256)
    expert_out = (pieces[:, 0] + pieces[:, 1]).astype(BF).reshape(512, 256)
    picked0 = dot(pick0.astype(BF), expert_out)
    picked1 = dot(pick1.astype(BF), expert_out)
    mixed = stream_v[...].astype(F32) + (gates[:, 0:1] * picked0 + gates[:, 1:2] * picked1)
    out[...] = mixed.astype(BF)

    wait_bytes(payload.at[0:15], p1_send.at[0])

    @pl.when(jnp.logical_not(p_self))
    def _():
        wait_bytes(payload.at[0], p1_send.at[1])

    wait_bytes(w_out, ws_sem.at[0])
    wait_bytes(gate_w.at[0], ws_sem.at[1])
    wait_bytes(up_w.at[0], ws_sem.at[2])
    wait_bytes(down_w.at[0], ws_sem.at[3])
    wait_bytes(heads_in.at[0], px_send.at[0])
    wait_bytes(heads_in.at[0], px_send.at[1])
    wait_bytes(heads_in.at[0, 0:2], px_send.at[2])
    wait_bytes(heads_in.at[0, 0:2], px_send.at[3])
    wait_bytes(final_in.at[0:7], rs_send.at[0])

    @pl.when(z_lo != core)
    def _():
        wait_bytes(payload.at[0:4], rs_send.at[1])

    wait_bytes(payload.at[0:7], d1_send.at[0])
    for dz in range(1, 4):
        wait_bytes(payload.at[0:8], d1_send.at[dz])
    for way in range(2):
        for i in range(4):
            wait_bytes(payload.at[0:8], d2_send.at[way, i])
            wait_bytes(payload.at[0:4], d3_send.at[way, i])
            wait_bytes(far_left.at[0], f_send.at[way, i])
            wait_bytes(from_left.at[0], g_send.at[way, i])
    wait_bytes(pre, ex_send.at[0])
    wait_bytes(squares, ex_send.at[1])
    for i in range(4):
        count = 7 if CHUNK_ORDER_OUT[i] == 0 else 8
        wait_bytes(payload.at[0:count], z_send.at[i])


def per_device(stream, heads_out, w_out, norm_gain, expert_ids, route_gates, w_gate, w_up, w_down):
    hbm = pl.BlockSpec(memory_space=pl.ANY)
    vmem = pl.BlockSpec(memory_space=pltpu.VMEM)
    dma = pltpu.SemaphoreType.DMA
    scratch = [
        pltpu.VMEM((4, 4, 4, 32, 256), BF),
        pltpu.VMEM((2, 1024, 256), BF),
        pltpu.VMEM((4, 2, 4, 32, 256), BF),
        pltpu.VMEM((8, 128, 256), BF),
        pltpu.VMEM((128, 256), BF),
        pltpu.VMEM((2, 16, 256, 256), BF),
        pltpu.VMEM((2, 16, 256, 256), BF),
        pltpu.VMEM((2, 16, 256, 256), BF),
        pltpu.VMEM((16, 32, 256), BF),
        pltpu.VMEM((4, 4, 8, 32, 256), BF),
        pltpu.VMEM((4, 256, 256), F32),
        pltpu.VMEM((4, 256, 256), F32),
        pltpu.VMEM((256, 128), F32),
        pltpu.VMEM((256, 128), F32),
        pltpu.VMEM((2, 256, 256), BF),
        pltpu.VMEM((4, 256, 256), BF),
        pltpu.VMEM((4, 256, 256), BF),
        pltpu.VMEM((4, 256, 256), BF),
        pltpu.VMEM((4, 128, 256), BF),
        pltpu.VMEM((4, 128, 256), BF),
        pltpu.VMEM((4, 256, 256), BF),
        pltpu.VMEM((4, 256, 256), BF),
        pltpu.VMEM((4, 8, 32, 256), BF),
        pltpu.VMEM((8, 4, 32, 256), BF),
        dma((1,)),
        dma((4,)),
        dma((4,)),
        dma((4,)),
        dma,
        dma((2,)),
        dma((4,)),
        dma((4,)),
        dma,
        dma((2,)),
        dma((4,)),
        dma((4,)),
        dma((2, 4)),
        dma((2, 4)),
        dma((2, 4)),
        dma((2, 4)),
        dma((2,)),
        dma((2,)),
        dma((2, 4)),
        dma((2, 4)),
        dma((2, 4)),
        dma((2, 4)),
        dma,
        dma((4,)),
    ]
    return pl.pallas_call(
        kernel,
        out_shape=jax.ShapeDtypeStruct((128, 256), BF),
        in_specs=[hbm, hbm, hbm, vmem, vmem, vmem, hbm, hbm, hbm],
        out_specs=vmem,
        scratch_shapes=scratch,
        compiler_params=pltpu.CompilerParams(
            has_side_effects=True, vmem_limit_bytes=48 * 1024 * 1024
        ),
        name="block",
    )(
        stream,
        heads_out,
        w_out,
        norm_gain.reshape(32, 1, 256),
        expert_ids,
        route_gates,
        w_gate.reshape(16, 2, 256, 256),
        w_up.reshape(16, 2, 256, 256),
        w_down,
    )


def solution(mesh):
    return jax.shard_map(
        per_device,
        mesh=mesh,
        in_specs=(
            P("row", "col"),
            P("row", "col"),
            P("row", "col"),
            P(),
            P("row", None),
            P("row", None),
            P(None, ("row", "col")),
            P(None, ("row", "col")),
            P(("row", "col"), None),
        ),
        out_specs=P("row", "col"),
        check_vma=False,
    )
```

time: 465 us -> 115 us (0.25)
  waiting for transfers between devices: 386 us -> 0 us
  Pallas kernels: 0 us -> 106 us
  other arithmetic: 22 us -> 0 us
  matrix products: 17.9 us -> 0 us
  between operations: 13.3 us -> 0.02 us
  starting transfers between devices: 9.5 us -> 0 us
  local copies, waits for them, and re-layouts: 15.1 us -> 7.86 us
    all_gather x3 -> x0, waiting for transfers between devices: 169 us -> none  [the longest x1 61.9 us: per_device(): heads_whole = lax.all_gather(heads_out, 'col', axis=1, tiled=True)]
    reduce_scatter x1 -> x0, waiting for transfers between devices: 117 us -> none  [per_device(): lax.psum_scatter(placed.astype(jnp.bfloat16), 'col', scatter_dimension=3,...]
    pallas_call x0 -> x1, Pallas kernels: none -> 106 us  [per_device(): pl.pallas_call(kernel, out_shape=jax.ShapeDtypeStruct((128, 256), BF), in...]
    all_to_all x2 -> x0, waiting for transfers between devices: 98.9 us -> none  [the longest x1 93.4 us: per_device(): lax.all_to_all(payload, 'row', split_axis=0, concat_axis=0, tiled=True)]
    dot_general x3 -> x0, matrix products: 17.9 us -> none  [the longest x1 12.4 us: per_device(): jnp.dot(activated, w_down, preferred_element_type=jnp.float32)]
    convert_element_type x6 -> x0, other arithmetic: 11 us -> none  [the longest x1 8.18 us: per_device(): placed.astype(jnp.bfloat16)]
    all_to_all x2 -> x0, starting transfers between devices: 9.19 us -> none  [the longest x1 5.04 us: per_device(): lax.all_to_all(payload, 'row', split_axis=0, concat_axis=0, tiled=True)]
    gather x3 -> x0, local copies, waits for them, and re-layouts: 9.03 us -> none  [the longest x1 7.82 us: per_device(): jnp.take(source, token_of_slot, axis=0) * filled[:, None]]
  transfers between devices with their start and end apart: 6 -> 0, of which waited for: 6 -> 0; matrix products, arithmetic and copies ran while one was open for 1% -> 0% of each run, Pallas kernels for 0% -> 0%
where the time goes in v1:
time: 115 us; the launch traced here: 113 us
  Pallas kernels  106 us (92%)
  local copies, waits for them, and re-layouts  7.86 us (7%)
    pallas_call x1, Pallas kernels, per_device(): pl.pallas_call(kernel, out_shape=jax.ShapeDtypeStruct((128, 256), BF), in...  106 us
    unnamed x13, local copies, waits for them, and re-layouts  7.86 us

profile of v1, /device:TPU:1, one launch (start us, length us, event | category | flops | bytes accessed | tf_op | source)
XLA Modules:
  0.0 113.4 jit_solution(591895426360811308)
XLA Ops:
  0.0 0.8 copy.10.ids
  0.8 0.8 copy.11.gates
  1.6 0.0 copy-start
  1.6 2.2 %copy-done = bf16[8192,256]{1,0:T(8,128)(2,1)S(1)} copy-done((bf16[8192,256]{1,0:T(8,128)(2,1)S(1)}, bf16[8192,256]{1,0:T(8,128)(2,1)}, u32[]{:S(2)}) %copy-start) | copy-done | bytes 4194328
  3.8 0.0 copy-start.1
  3.8 1.0 copy-done.1
  4.8 0.0 copy-start.2
  4.8 0.8 copy-done.2
  5.6 0.0 copy-start.3
  5.6 0.8 copy-done.3
  6.5 0.0 copy-start.4
  6.5 0.8 copy-done.4
  7.2 105.6 %block.1 = bf16[128,256]{1,0:T(8,128)(2,1)S(1)} custom-call(bf16[128,256]{1,0:T(8,128)(2,1)S(1)} %copy-done.2, bf16[128,256]{1,0:T(8,128)(2,1)S(1)} %copy-done.3, bf16[1024,256]{1,0:T(8,128)(2,1)S(1)} %copy-done.1, f32[32,1,256]{2,1,0:T(1,128)S(1)} %bitcast.4, s32[128,2]{1,0:T(8,128)S(1)} %copy.10.ids, f32[128,2]{1,0:T(8,128)S(1)} %copy.11.gates, ...), custom_call_target="tpu_custom_call" | custom-call | tf_op jit(solution)/shard_map/block/pallas_call | solution.py:411
  112.8 0.6 copy.13
Async XLA Ops:
  1.6 2.2 %copy-start = (bf16[8192,256]{1,0:T(8,128)(2,1)S(1)}, bf16[8192,256]{1,0:T(8,128)(2,1)}, u32[]{:S(2)}) copy-start(bf16[8192,256]{1,0:T(8,128)(2,1)} %param.15) | copy-start | bytes 12582916
  3.8 1.0 copy-start.1
  4.8 0.8 copy-start.2
  5.6 0.8 copy-start.3
  6.5 0.8 copy-start.4

commit v2 on v1

--- a/solution.py
+++ b/solution.py
@@ -43,9 +43,10 @@
 
 
 def kernel(
-    stream, heads, w_out, gain, ids, gates, w_gate, w_up, w_down,
+    stream, heads, w_out, gain_hbm, ids_hbm, gates_hbm, w_gate, w_up, w_down,
     out,
     heads_in, w_out_pair, proj_out, proj_in, stream_v, gate_w, up_w, down_w,
+    gain, ids, gates, spread, pick, gate_col,
     payload, tokens, pre, pre_in, squares, squares_in, act,
     far_out, right_out, left_out, far_left, far_right, from_left, from_right, summed, final_in,
     in_sem, w_sem, wr_sem, ws_sem,
@@ -63,14 +64,56 @@
     right = lax.rem(x + 1, 4)
     left = lax.rem(x + 3, 4)
     far = lax.rem(x + 2, 4)
+    closers = []
+
+    def finish():
+        for close in closers:
+            close()
+
+    def later(view, sem):
+        closers.append(lambda: wait_bytes(view, sem))
+
+    def later_if(condition, view, sem):
+        def close():
+            @pl.when(condition)
+            def _():
+                wait_bytes(view, sem)
+
+        closers.append(close)
+
     right_dev = place(z_lo, y, z_hi, right, core)
     left_dev = place(z_lo, y, z_hi, left, core)
     pair_dev = place(z_lo, y, z_hi, x, other)
 
-    own_group = lax.rem(x, 2) * 2 + core
+    barrier = pltpu.get_barrier_semaphore()
     p_row_lo = lax.div(z_hi, 2)
     p_row_y = lax.rem(z_hi, 2) * 2 + lax.div(x, 2)
     p_self = jnp.logical_and(jnp.logical_and(p_row_lo == z_lo, p_row_y == y), z_lo == core)
+    rs_self = z_lo == core
+
+    def greet(device):
+        pl.semaphore_signal(barrier, inc=1, device_id=device, device_id_type=MESH)
+
+    def greet_other(device):
+        @pl.when(jnp.logical_or(device[0] != row, device[1] != col))
+        def _():
+            greet(device)
+
+    greet(right_dev)
+    greet(left_dev)
+    greet(pair_dev)
+    for from_y in range(4):
+        for from_x in range(2):
+            for from_core in range(2):
+                greet_other(
+                    place(core, from_y, 2 * z_lo + lax.div(y, 2), 2 * lax.rem(y, 2) + from_x, from_core)
+                )
+    for from_lo in range(2):
+        for from_y in range(4):
+            greet_other(place(from_lo, from_y, z_hi, x, z_lo))
+    pl.semaphore_wait(barrier, 27 - p_self.astype(jnp.int32) - rs_self.astype(jnp.int32))
+
+    own_group = lax.rem(x, 2) * 2 + core
     for dz in (2, 1, 3, 0):
         for dx in (2, 1, 3, 0):
             to_x = lax.rem(x + dx, 4)
@@ -89,9 +132,15 @@
             else:
                 send(src, dst, p1_send.at[0], p1_recv, device)
 
+    later(payload.at[0:15], p1_send.at[0])
+    later_if(jnp.logical_not(p_self), payload.at[0], p1_send.at[1])
+
     local_copy(w_out, w_out_pair.at[core], w_sem.at[0])
     send(w_out, w_out_pair.at[core], ws_sem.at[0], wr_sem.at[0], pair_dev)
+    local_copy(ids_hbm, ids, in_sem.at[1])
+    local_copy(gates_hbm, gates, in_sem.at[2])
     local_copy(stream, stream_v, in_sem.at[0])
+    local_copy(gain_hbm, gain, in_sem.at[3])
     local_copy(w_gate.at[:, core], gate_w.at[core], w_sem.at[1])
     local_copy(w_up.at[:, core], up_w.at[core], w_sem.at[2])
     send(w_gate.at[:, other], gate_w.at[core], ws_sem.at[1], wr_sem.at[1], pair_dev)
@@ -105,18 +154,29 @@
         return carry
 
     lax.fori_loop(0, 16, load_down, 0)
-
+    later(w_out, ws_sem.at[0])
+    later(gate_w.at[0], ws_sem.at[1])
+    later(up_w.at[0], ws_sem.at[2])
+    later(down_w.at[0], ws_sem.at[3])
+
+    wait_bytes(ids, in_sem.at[1])
+    wait_bytes(gates, in_sem.at[2])
+    expert_sub = lax.broadcasted_iota(jnp.int32, (16, 128), 0)
     lane = lax.broadcasted_iota(jnp.int32, (128, 128), 1)
     sub = lax.broadcasted_iota(jnp.int32, (128, 128), 0)
-    first = (ids[:, 0:1] == lane).astype(F32)
-    second = (ids[:, 1:2] == lane).astype(F32)
-    earlier = dot((lane < sub).astype(BF), (first + second).astype(BF))
-    slot_lane = lax.broadcasted_iota(jnp.int32, (128, 512), 1)
-    slot0 = ids[:, 0:1] * 32 + jnp.sum(earlier * first, axis=1, keepdims=True).astype(jnp.int32)
-    slot1 = ids[:, 1:2] * 32 + jnp.sum(earlier * second, axis=1, keepdims=True).astype(jnp.int32)
-    pick0 = (slot0 == slot_lane).astype(F32)
-    pick1 = (slot1 == slot_lane).astype(F32)
-    spread = (pick0 + pick1).T.astype(BF)
+    first = (ids[0:1, :] == expert_sub).astype(F32)
+    second = (ids[1:2, :] == expert_sub).astype(F32)
+    earlier = dot((first + second).astype(BF), (sub < lane).astype(BF))
+    slot_sub = lax.broadcasted_iota(jnp.int32, (512, 128), 0)
+    slot0 = ids[0:1, :] * 32 + jnp.sum(earlier * first, axis=0, keepdims=True).astype(jnp.int32)
+    slot1 = ids[1:2, :] * 32 + jnp.sum(earlier * second, axis=0, keepdims=True).astype(jnp.int32)
+    match0 = (slot0 == slot_sub).astype(F32)
+    match1 = (slot1 == slot_sub).astype(F32)
+    spread[...] = (match0 + match1).astype(BF)
+    pick[0] = match0.T.astype(BF)
+    pick[1] = match1.T.astype(BF)
+    for k in range(2):
+        gate_col[k] = jnp.broadcast_to(gates[k:k + 1, :], (128, 128)).T
     pre[...] = jnp.zeros_like(pre)
     squares[...] = jnp.zeros_like(squares)
 
@@ -136,17 +196,23 @@
                 dst = proj_in.at[row, pl.ds(group * 32, 32), :]
                 device = place(core, to_y, z_hi, x, c)
                 if dy == 0 and dc == 0:
-                    @pl.when(z_lo == core)
+                    @pl.when(rs_self)
                     def _():
                         local_copy(src, dst, rs_recv)
 
-                    @pl.when(z_lo != core)
+                    @pl.when(jnp.logical_not(rs_self))
                     def _():
                         send(src, dst, rs_send.at[1], rs_recv, device)
                 else:
                     send(src, dst, rs_send.at[0], rs_recv, device)
 
     wait_bytes(heads_in.at[x], p1_recv)
+    later(heads_in.at[0], px_send.at[0])
+    later(heads_in.at[0], px_send.at[1])
+    later(heads_in.at[0, 0:2], px_send.at[2])
+    later(heads_in.at[0, 0:2], px_send.at[3])
+    later(final_in.at[0:7], rs_send.at[0])
+    later_if(jnp.logical_not(rs_self), payload.at[0:4], rs_send.at[1])
     send(heads_in.at[x], heads_in.at[x], px_send.at[0], px_recv.at[0], right_dev)
     send(heads_in.at[x], heads_in.at[x], px_send.at[1], px_recv.at[1], left_dev)
     wait_bytes(w_out_pair.at[core], w_sem.at[0])
@@ -168,8 +234,10 @@
     for r in range(8):
         residual = residual + proj_in[r].astype(F32)
     stream_v[...] = residual.astype(BF)
-
-    payload[...] = dot(spread, stream_v[...]).astype(BF).reshape(16, 32, 256)
+    for dz in range(4):
+        later(payload.at[0:7 if dz == 0 else 8], d1_send.at[dz])
+
+    payload[...] = dot(spread[...], stream_v[...]).astype(BF).reshape(16, 32, 256)
     for dz in CHUNK_ORDER_IN:
         to_z = lax.rem(z_hi + dz, 4)
         for dl in (1, 0):
@@ -184,6 +252,7 @@
                 else:
                     send(src, dst, d1_send.at[dz], d1_recv.at[dz], place(to_lo, to_y, to_z, x, core))
 
+    wait_bytes(gain, in_sem.at[3])
     wait_bytes(gate_w.at[core], w_sem.at[1])
     wait_bytes(up_w.at[core], w_sem.at[2])
     wait_bytes(gate_w.at[other], wr_sem.at[1])
@@ -227,6 +296,10 @@
         wait_bytes(tokens.at[far, zc, 4:8], d3_recv.at[1, i])
         absorb(far, zc)
 
+    for way in range(2):
+        for i in range(4):
+            later(payload.at[0:8], d2_send.at[way, i])
+            later(payload.at[0:4], d3_send.at[way, i])
     for i in range(6):
         if i < 4:
             gather_first(i)
@@ -234,6 +307,9 @@
             gather_second(i - 1)
         if i >= 2:
             gather_third(i - 2)
+
+    later(pre, ex_send.at[0])
+    later(squares, ex_send.at[1])
 
     send(pre, pre_in, ex_send.at[0], ex_recv.at[0], pair_dev)
     send(squares, squares_in, ex_send.at[1], ex_recv.at[1], pair_dev)
@@ -297,6 +373,12 @@
                 else:
                     send(src, dst, z_send.at[i], z_recv, place(to_lo, to_y, zc, x, core))
 
+    for way in range(2):
+        for i in range(4):
+            later(far_left.at[0], f_send.at[way, i])
+            later(from_left.at[0], g_send.at[way, i])
+    for i in range(4):
+        later(payload.at[0:7 if CHUNK_ORDER_OUT[i] == 0 else 8], z_send.at[i])
     return_first(0)
     return_first(1)
     return_second(0)
@@ -313,45 +395,13 @@
     wait_bytes(final_in, z_recv)
     pieces = final_in[...].astype(F32).reshape(16, 2, 32, 256)
     expert_out = (pieces[:, 0] + pieces[:, 1]).astype(BF).reshape(512, 256)
-    picked0 = dot(pick0.astype(BF), expert_out)
-    picked1 = dot(pick1.astype(BF), expert_out)
-    mixed = stream_v[...].astype(F32) + (gates[:, 0:1] * picked0 + gates[:, 1:2] * picked1)
+    picked0 = dot(pick[0], expert_out)
+    picked1 = dot(pick[1], expert_out)
+    mixed = stream_v[...].astype(F32) + (
+        gate_col[0, :, 0:1] * picked0 + gate_col[1, :, 0:1] * picked1
+    )
     out[...] = mixed.astype(BF)
-
-    wait_bytes(payload.at[0:15], p1_send.at[0])
-
-    @pl.when(jnp.logical_not(p_self))
-    def _():
-        wait_bytes(payload.at[0], p1_send.at[1])
-
-    wait_bytes(w_out, ws_sem.at[0])
-    wait_bytes(gate_w.at[0], ws_sem.at[1])
-    wait_bytes(up_w.at[0], ws_sem.at[2])
-    wait_bytes(down_w.at[0], ws_sem.at[3])
-    wait_bytes(heads_in.at[0], px_send.at[0])
-    wait_bytes(heads_in.at[0], px_send.at[1])
-    wait_bytes(heads_in.at[0, 0:2], px_send.at[2])
-    wait_bytes(heads_in.at[0, 0:2], px_send.at[3])
-    wait_bytes(final_in.at[0:7], rs_send.at[0])
-
-    @pl.when(z_lo != core)
-    def _():
-        wait_bytes(payload.at[0:4], rs_send.at[1])
-
-    wait_bytes(payload.at[0:7], d1_send.at[0])
-    for dz in range(1, 4):
-        wait_bytes(payload.at[0:8], d1_send.at[dz])
-    for way in range(2):
-        for i in range(4):
-            wait_bytes(payload.at[0:8], d2_send.at[way, i])
-            wait_bytes(payload.at[0:4], d3_send.at[way, i])
-            wait_bytes(far_left.at[0], f_send.at[way, i])
-            wait_bytes(from_left.at[0], g_send.at[way, i])
-    wait_bytes(pre, ex_send.at[0])
-    wait_bytes(squares, ex_send.at[1])
-    for i in range(4):
-        count = 7 if CHUNK_ORDER_OUT[i] == 0 else 8
-        wait_bytes(payload.at[0:count], z_send.at[i])
+    finish()
 
 
 def per_device(stream, heads_out, w_out, norm_gain, expert_ids, route_gates, w_gate, w_up, w_down):
@@ -367,6 +417,12 @@
         pltpu.VMEM((2, 16, 256, 256), BF),
         pltpu.VMEM((2, 16, 256, 256), BF),
         pltpu.VMEM((2, 16, 256, 256), BF),
+        pltpu.VMEM((32, 1, 256), F32),
+        pltpu.VMEM((2, 128), jnp.int32),
+        pltpu.VMEM((2, 128), F32),
+        pltpu.VMEM((512, 128), BF),
+        pltpu.VMEM((2, 128, 512), BF),
+        pltpu.VMEM((2, 128, 128), F32),
         pltpu.VMEM((16, 32, 256), BF),
         pltpu.VMEM((4, 4, 8, 32, 256), BF),
         pltpu.VMEM((4, 256, 256), F32),
@@ -383,7 +439,7 @@
         pltpu.VMEM((4, 256, 256), BF),
         pltpu.VMEM((4, 8, 32, 256), BF),
         pltpu.VMEM((8, 4, 32, 256), BF),
-        dma((1,)),
+        dma((4,)),
         dma((4,)),
         dma((4,)),
         dma((4,)),
@@ -411,11 +467,11 @@
     return pl.pallas_call(
         kernel,
         out_shape=jax.ShapeDtypeStruct((128, 256), BF),
-        in_specs=[hbm, hbm, hbm, vmem, vmem, vmem, hbm, hbm, hbm],
+        in_specs=[hbm] * 9,
         out_specs=vmem,
         scratch_shapes=scratch,
         compiler_params=pltpu.CompilerParams(
-            has_side_effects=True, vmem_limit_bytes=48 * 1024 * 1024
+            collective_id=0, has_side_effects=True, vmem_limit_bytes=60 * 1024 * 1024
         ),
         name="block",
     )(
@@ -423,8 +479,8 @@
         heads_out,
         w_out,
         norm_gain.reshape(32, 1, 256),
-        expert_ids,
-        route_gates,
+        expert_ids.T,
+        route_gates.T,
         w_gate.reshape(16, 2, 256, 256),
         w_up.reshape(16, 2, 256, 256),
         w_down,

time: 115 us -> 100 us (0.87); the launches traced: 113 us -> 100 us
  Pallas kernels: 106 us -> 98.5 us
  local copies, waits for them, and re-layouts: 7.86 us -> 1.47 us
    pallas_call x1, Pallas kernels: 106 us -> 98.5 us  [per_device(): pl.pallas_call(kernel, out_shape=jax.ShapeDtypeStruct((128, 256), BF), in...]
    unnamed x13 -> x1, local copies, waits for them, and re-layouts: 7.86 us -> 1.47 us
where the time goes in v2:
time: 100 us
  Pallas kernels  98.5 us (98%)
  local copies, waits for them, and re-layouts  1.47 us (1%)
    pallas_call x1, Pallas kernels, per_device(): pl.pallas_call(kernel, out_shape=jax.ShapeDtypeStruct((128, 256), BF), in...  98.5 us

profile of v2, /device:TPU:1, one launch (start us, length us, event | category | flops | bytes accessed | tf_op | source)
XLA Modules:
  0.0 100.0 jit_solution(1745543642243876107)
XLA Ops:
  0.0 98.5 %block.1 = bf16[128,256]{1,0:T(8,128)(2,1)} custom-call(bf16[128,256]{1,0:T(8,128)(2,1)} %stream.1, bf16[128,256]{1,0:T(8,128)(2,1)} %heads.1, bf16[1024,256]{1,0:T(8,128)(2,1)} %w_out.1, f32[32,1,256]{2,1,0:T(1,128)} %bitcast.7, s32[2,128]{1,0:T(2,128)} %bitcast.8, f32[2,128]{1,0:T(2,128)} %bitcast.9, bf16[16,2,256,256]{3,2,1,0:T(8,128)(2,1)} %bitcast.5, ...), custom_call_target="tpu_custom_call" | custom-call | tf_op jit(solution)/shard_map/block/pallas_call | solution.py:467
  98.5 1.5 %copy.11 = bf16[128,256]{1,0:T(8,128)(2,1)} copy(bf16[128,256]{1,0:T(8,128)(2,1)} %block.1) | data formatting | bytes 131072

commit v3 on v2

--- a/solution.py
+++ b/solution.py
@@ -11,6 +11,25 @@
 WIDTH = 8192
 CHUNK_ORDER_IN = (0, 1, 3, 2)
 CHUNK_ORDER_OUT = (2, 1, 3, 0)
+Y_STEPS = ((1, 3), (0, 2))
+PARTS = len(Y_STEPS)
+BLOCKS = tuple(2 * len(part) for part in Y_STEPS)
+MOST = max(BLOCKS)
+PLAN = (
+    (
+        "d00", "d01", "d03", "d02",
+    ),
+    (
+        "p00", "p01", "p02", "p03", "d10", "d11", "d13", "d12", "q00", "q01", "q02", "q03",
+        "r00", "r01", "r02", "r03", "e0", "p10", "p11", "p12", "p13", "q10", "q11", "q12",
+        "q13", "f0",
+    ),
+    (
+        "a00", "a01", "a02", "a03", "r10", "r11", "r12", "r13", "e1", "b00", "b01", "b02",
+        "b03", "f1", "a10", "a11", "c00", "c01", "b10", "a12", "b11", "a13", "c02", "c03",
+        "c10", "b12", "c11", "b13", "c12", "c13",
+    ),
+)
 
 
 def place(z_lo, y, z_hi, x, core):
@@ -48,7 +67,7 @@
     heads_in, w_out_pair, proj_out, proj_in, stream_v, gate_w, up_w, down_w,
     gain, ids, gates, spread, pick, gate_col,
     payload, tokens, pre, pre_in, squares, squares_in, act,
-    far_out, right_out, left_out, far_left, far_right, from_left, from_right, summed, final_in,
+    far_out, right_out, left_out, kept, far_left, far_right, from_left, from_right, summed, final_in,
     in_sem, w_sem, wr_sem, ws_sem,
     p1_recv, p1_send, px_recv, px_send, rs_recv, rs_send,
     d1_recv, d1_send, d2_recv, d2_send, d3_recv, d3_send, ex_recv, ex_send,
@@ -207,25 +226,30 @@
                     send(src, dst, rs_send.at[0], rs_recv, device)
 
     wait_bytes(heads_in.at[x], p1_recv)
-    later(heads_in.at[0], px_send.at[0])
-    later(heads_in.at[0], px_send.at[1])
-    later(heads_in.at[0, 0:2], px_send.at[2])
-    later(heads_in.at[0, 0:2], px_send.at[3])
     later(final_in.at[0:7], rs_send.at[0])
     later_if(jnp.logical_not(rs_self), payload.at[0:4], rs_send.at[1])
-    send(heads_in.at[x], heads_in.at[x], px_send.at[0], px_recv.at[0], right_dev)
-    send(heads_in.at[x], heads_in.at[x], px_send.at[1], px_recv.at[1], left_dev)
+    ends = (heads_in.at[x, 0:2], heads_in.at[x, 2:4])
+    for k in range(2):
+        send(ends[k], ends[k], px_send.at[0, k], px_recv.at[0, k], right_dev)
+        send(ends[1 - k], ends[1 - k], px_send.at[1, k], px_recv.at[1, k], left_dev)
     wait_bytes(w_out_pair.at[core], w_sem.at[0])
     wait_bytes(w_out_pair.at[other], wr_sem.at[0])
     project(x)
-    wait_bytes(heads_in.at[left], px_recv.at[0])
-    send(heads_in.at[left, 0:2], heads_in.at[left, 0:2], px_send.at[2], px_recv.at[2], right_dev)
-    wait_bytes(heads_in.at[right], px_recv.at[1])
-    send(heads_in.at[right, 2:4], heads_in.at[right, 2:4], px_send.at[3], px_recv.at[3], left_dev)
+    view = heads_in.at[left, 0:2]
+    wait_bytes(view, px_recv.at[0, 0])
+    send(view, view, px_send.at[0, 2], px_recv.at[0, 2], right_dev)
+    view = heads_in.at[right, 2:4]
+    wait_bytes(view, px_recv.at[1, 0])
+    send(view, view, px_send.at[1, 2], px_recv.at[1, 2], left_dev)
+    for way in range(2):
+        for k in range(3):
+            later(heads_in.at[0, 0:2], px_send.at[way, k])
+    wait_bytes(heads_in.at[left, 2:4], px_recv.at[0, 1])
     project(left)
+    wait_bytes(heads_in.at[right, 0:2], px_recv.at[1, 1])
     project(right)
-    wait_bytes(heads_in.at[far, 0:2], px_recv.at[2])
-    wait_bytes(heads_in.at[far, 2:4], px_recv.at[3])
+    wait_bytes(heads_in.at[far, 0:2], px_recv.at[0, 2])
+    wait_bytes(heads_in.at[far, 2:4], px_recv.at[1, 2])
     project(far)
 
     wait_bytes(stream_v, in_sem.at[0])
@@ -234,163 +258,177 @@
     for r in range(8):
         residual = residual + proj_in[r].astype(F32)
     stream_v[...] = residual.astype(BF)
-    for dz in range(4):
-        later(payload.at[0:7 if dz == 0 else 8], d1_send.at[dz])
-
     payload[...] = dot(spread[...], stream_v[...]).astype(BF).reshape(16, 32, 256)
-    for dz in CHUNK_ORDER_IN:
+
+    def dispatch(h, dz):
         to_z = lax.rem(z_hi + dz, 4)
-        for dl in (1, 0):
-            to_lo = z_lo if dl == 0 else 1 - z_lo
-            for dy in (2, 1, 3, 0):
-                to_y = lax.rem(y + dy, 4)
+        for step, dy in enumerate(Y_STEPS[h]):
+            to_y = lax.rem(y + dy, 4)
+            for dl in (1, 0):
+                to_lo = z_lo if dl == 0 else 1 - z_lo
                 expert = 2 * (to_lo * 4 + to_y) + lax.div(to_z, 2)
                 src = payload.at[expert]
-                dst = tokens.at[x, z_hi, row]
+                dst = tokens.at[h, x, z_hi, step * 2 + z_lo]
                 if dz == 0 and dl == 0 and dy == 0:
-                    local_copy(src, dst, d1_recv.at[dz])
+                    local_copy(src, dst, d1_recv.at[h, dz])
                 else:
-                    send(src, dst, d1_send.at[dz], d1_recv.at[dz], place(to_lo, to_y, to_z, x, core))
-
-    wait_bytes(gain, in_sem.at[3])
-    wait_bytes(gate_w.at[core], w_sem.at[1])
-    wait_bytes(up_w.at[core], w_sem.at[2])
-    wait_bytes(gate_w.at[other], wr_sem.at[1])
-    wait_bytes(up_w.at[other], wr_sem.at[2])
-
-    def absorb(from_x, from_z):
-        block = tokens[from_x, from_z].reshape(256, 256).astype(F32)
+                    send(src, dst, d1_send.at[h, dz], d1_recv.at[h, dz], place(to_lo, to_y, to_z, x, core))
+        later(payload.at[0:BLOCKS[h] - (dz == 0 and 0 in Y_STEPS[h])], d1_send.at[h, dz])
+
+    def absorb(h, from_x, from_z):
+        n = BLOCKS[h] * 32
+        block = tokens[h, from_x, from_z, 0:BLOCKS[h]].reshape(n, 256).astype(F32)
         square = block * block
-        squares[...] += square[:, 0:128] + square[:, 128:256]
+        squares[h, 0:n] += square[:, 0:128] + square[:, 128:256]
         scaled = (block * gain[from_z * 8 + from_x * 2 + core]).astype(BF)
         b = from_z * 4 + from_x
         for c in range(2):
-            pre[c] += dot(scaled, gate_w[c, b])
-            pre[2 + c] += dot(scaled, up_w[c, b])
+            pre[h, c, 0:n] += dot(scaled, gate_w[c, b])
+            pre[h, 2 + c, 0:n] += dot(scaled, up_w[c, b])
 
     def chunk_z(i):
         return lax.rem(z_hi + 4 - CHUNK_ORDER_IN[i], 4)
 
-    def gather_first(i):
+    def gather_first(h, i):
         zc = chunk_z(i)
-        wait_bytes(tokens.at[x, zc], d1_recv.at[CHUNK_ORDER_IN[i]])
-        view = tokens.at[x, zc]
-        send(view, view, d2_send.at[0, i], d2_recv.at[0, i], right_dev)
-        send(view, view, d2_send.at[1, i], d2_recv.at[1, i], left_dev)
-        absorb(x, zc)
-
-    def gather_second(i):
+        n = BLOCKS[h]
+        wait_bytes(tokens.at[h, x, zc, 0:n], d1_recv.at[h, CHUNK_ORDER_IN[i]])
+        ends = (tokens.at[h, x, zc, 0:n // 2], tokens.at[h, x, zc, n // 2:n])
+        for k in range(2):
+            send(ends[k], ends[k], d2_send.at[h, 0, i, k], d2_recv.at[h, 0, i, k], right_dev)
+            send(ends[1 - k], ends[1 - k], d2_send.at[h, 1, i, k], d2_recv.at[h, 1, i, k], left_dev)
+            for way in range(2):
+                later(payload.at[0:n // 2], d2_send.at[h, way, i, k])
+        absorb(h, x, zc)
+
+    def gather_second(h, i):
         zc = chunk_z(i)
-        wait_bytes(tokens.at[left, zc], d2_recv.at[0, i])
-        view = tokens.at[left, zc, 0:4]
-        send(view, view, d3_send.at[0, i], d3_recv.at[0, i], right_dev)
-        wait_bytes(tokens.at[right, zc], d2_recv.at[1, i])
-        view = tokens.at[right, zc, 4:8]
-        send(view, view, d3_send.at[1, i], d3_recv.at[1, i], left_dev)
-        absorb(left, zc)
-        absorb(right, zc)
-
-    def gather_third(i):
+        n = BLOCKS[h]
+        view = tokens.at[h, left, zc, 0:n // 2]
+        wait_bytes(view, d2_recv.at[h, 0, i, 0])
+        send(view, view, d3_send.at[h, 0, i], d3_recv.at[h, 0, i], right_dev)
+        view = tokens.at[h, right, zc, n // 2:n]
+        wait_bytes(view, d2_recv.at[h, 1, i, 0])
+        send(view, view, d3_send.at[h, 1, i], d3_recv.at[h, 1, i], left_dev)
+        for way in range(2):
+            later(payload.at[0:n // 2], d3_send.at[h, way, i])
+        wait_bytes(tokens.at[h, left, zc, n // 2:n], d2_recv.at[h, 0, i, 1])
+        absorb(h, left, zc)
+        wait_bytes(tokens.at[h, right, zc, 0:n // 2], d2_recv.at[h, 1, i, 1])
+        absorb(h, right, zc)
+
+    def gather_third(h, i):
         zc = chunk_z(i)
-        wait_bytes(tokens.at[far, zc, 0:4], d3_recv.at[0, i])
-        wait_bytes(tokens.at[far, zc, 4:8], d3_recv.at[1, i])
-        absorb(far, zc)
-
-    for way in range(2):
-        for i in range(4):
-            later(payload.at[0:8], d2_send.at[way, i])
-            later(payload.at[0:4], d3_send.at[way, i])
-    for i in range(6):
-        if i < 4:
-            gather_first(i)
-        if 1 <= i < 5:
-            gather_second(i - 1)
-        if i >= 2:
-            gather_third(i - 2)
-
-    later(pre, ex_send.at[0])
-    later(squares, ex_send.at[1])
-
-    send(pre, pre_in, ex_send.at[0], ex_recv.at[0], pair_dev)
-    send(squares, squares_in, ex_send.at[1], ex_recv.at[1], pair_dev)
-    wait_bytes(squares_in, ex_recv.at[1])
-    wait_bytes(pre_in, ex_recv.at[0])
-    mean = jnp.sum(squares[...] + squares_in[...], axis=1, keepdims=True) / WIDTH
-    scale = lax.rsqrt(mean + 1e-05)
-    for c in range(2):
-        gate_pre = (pre[c] + pre_in[c]) * scale
-        up_pre = (pre[2 + c] + pre_in[2 + c]) * scale
-        act[c] = (gate_pre / (1.0 + jnp.exp(-gate_pre)) * up_pre).astype(BF)
-
-    wait_bytes(down_w.at[core], w_sem.at[3])
-    wait_bytes(down_w.at[other], wr_sem.at[3])
-
-    def down(start, rows, to_x, zc):
+        n = BLOCKS[h]
+        wait_bytes(tokens.at[h, far, zc, 0:n // 2], d3_recv.at[h, 0, i])
+        wait_bytes(tokens.at[h, far, zc, n // 2:n], d3_recv.at[h, 1, i])
+        absorb(h, far, zc)
+
+    def exchange_first(h):
+        n = BLOCKS[h] * 32
+        sent, landed = pre.at[h, :, 0:n], pre_in.at[h, :, 0:n]
+        send(sent, landed, ex_send.at[h, 0], ex_recv.at[h, 0], pair_dev)
+        later(sent, ex_send.at[h, 0])
+        sent, landed = squares.at[h, 0:n], squares_in.at[h, 0:n]
+        send(sent, landed, ex_send.at[h, 1], ex_recv.at[h, 1], pair_dev)
+        later(sent, ex_send.at[h, 1])
+
+    def exchange_second(h):
+        n = BLOCKS[h] * 32
+        wait_bytes(squares_in.at[h, 0:n], ex_recv.at[h, 1])
+        wait_bytes(pre_in.at[h, :, 0:n], ex_recv.at[h, 0])
+        mean = jnp.sum(squares[h, 0:n] + squares_in[h, 0:n], axis=1, keepdims=True) / WIDTH
+        scale = lax.rsqrt(mean + 1e-05)
+        for c in range(2):
+            gate_pre = (pre[h, c, 0:n] + pre_in[h, c, 0:n]) * scale
+            up_pre = (pre[h, 2 + c, 0:n] + pre_in[h, 2 + c, 0:n]) * scale
+            act[h, c, 0:n] = (gate_pre / (1.0 + jnp.exp(-gate_pre)) * up_pre).astype(BF)
+
+    def down(h, to_x, zc):
         b = zc * 4 + to_x
-        return dot(act[0, start:start + rows, :], down_w[0, b]) + dot(
-            act[1, start:start + rows, :], down_w[1, b]
-        )
+        n = BLOCKS[h] * 32
+        return dot(act[h, 0, 0:n], down_w[0, b]) + dot(act[h, 1, 0:n], down_w[1, b])
 
     def out_z(i):
         return lax.rem(z_hi + CHUNK_ORDER_OUT[i], 4)
 
-    def return_first(i):
+    def return_first(h, i):
         zc = out_z(i)
-        far_out[i] = down(0, 256, far, zc).astype(BF)
-        send(far_out.at[i, 0:128], far_left.at[i], f_send.at[0, i], f_recv.at[0, i], right_dev)
-        send(far_out.at[i, 128:256], far_right.at[i], f_send.at[1, i], f_recv.at[1, i], left_dev)
-        right_out[i, 128:256] = down(128, 128, right, zc).astype(BF)
-        send(right_out.at[i, 128:256], from_left.at[i, 128:256], g_send.at[0, i], g_recv.at[0, i], right_dev)
-        left_out[i, 0:128] = down(0, 128, left, zc).astype(BF)
-        send(left_out.at[i, 0:128], from_right.at[i, 0:128], g_send.at[1, i], g_recv.at[1, i], left_dev)
-
-    def return_second(i):
+        n = BLOCKS[h] * 32
+        m = n // 2
+        far_out[h, i, 0:n] = down(h, far, zc).astype(BF)
+        send(far_out.at[h, i, 0:m], far_left.at[h, i, 0:m], f_send.at[h, 0, i], f_recv.at[h, 0, i], right_dev)
+        send(far_out.at[h, i, m:n], far_right.at[h, i, 0:m], f_send.at[h, 1, i], f_recv.at[h, 1, i], left_dev)
+        mine = down(h, right, zc)
+        right_out[h, i, m:n] = mine[m:n].astype(BF)
+        send(right_out.at[h, i, m:n], from_left.at[h, i, m:n], g_send.at[h, 0, i], g_recv.at[h, 0, i], right_dev)
+        kept[h, i, 0, 0:m] = mine[0:m]
+        mine = down(h, left, zc)
+        left_out[h, i, 0:m] = mine[0:m].astype(BF)
+        send(left_out.at[h, i, 0:m], from_right.at[h, i, 0:m], g_send.at[h, 1, i], g_recv.at[h, 1, i], left_dev)
+        kept[h, i, 1, 0:m] = mine[m:n]
+        for way in range(2):
+            later(far_left.at[h, i, 0:m], f_send.at[h, way, i])
+
+    def return_second(h, i):
+        n = BLOCKS[h] * 32
+        m = n // 2
+        wait_bytes(far_left.at[h, i, 0:m], f_recv.at[h, 0, i])
+        right_out[h, i, 0:m] = (kept[h, i, 0, 0:m] + far_left[h, i, 0:m].astype(F32)).astype(BF)
+        send(right_out.at[h, i, 0:m], from_left.at[h, i, 0:m], g_send.at[h, 0, i], g_recv.at[h, 0, i], right_dev)
+        wait_bytes(far_right.at[h, i, 0:m], f_recv.at[h, 1, i])
+        left_out[h, i, m:n] = (kept[h, i, 1, 0:m] + far_right[h, i, 0:m].astype(F32)).astype(BF)
+        send(left_out.at[h, i, m:n], from_right.at[h, i, m:n], g_send.at[h, 1, i], g_recv.at[h, 1, i], left_dev)
+        for way in range(2):
+            later(from_left.at[h, i, 0:n], g_send.at[h, way, i])
+
+    def return_third(h, i):
         zc = out_z(i)
-        mine = down(0, 128, right, zc)
-        wait_bytes(far_left.at[i], f_recv.at[0, i])
-        right_out[i, 0:128] = (mine + far_left[i].astype(F32)).astype(BF)
-        send(right_out.at[i, 0:128], from_left.at[i, 0:128], g_send.at[0, i], g_recv.at[0, i], right_dev)
-        mine = down(128, 128, left, zc)
-        wait_bytes(far_right.at[i], f_recv.at[1, i])
-        left_out[i, 128:256] = (mine + far_right[i].astype(F32)).astype(BF)
-        send(left_out.at[i, 128:256], from_right.at[i, 128:256], g_send.at[1, i], g_recv.at[1, i], left_dev)
-
-    def return_third(i):
-        zc = out_z(i)
-        mine = down(0, 256, x, zc)
-        wait_bytes(from_left.at[i], g_recv.at[0, i])
-        wait_bytes(from_right.at[i], g_recv.at[1, i])
-        total = mine + from_left[i].astype(F32) + from_right[i].astype(F32)
-        summed[i] = total.astype(BF).reshape(8, 32, 256)
-        for dl in (1, 0):
-            to_lo = z_lo if dl == 0 else 1 - z_lo
-            for dy in (2, 1, 3, 0):
-                to_y = lax.rem(y + dy, 4)
-                src = summed.at[i, to_lo * 4 + to_y]
+        n = BLOCKS[h] * 32
+        mine = down(h, x, zc)
+        wait_bytes(from_left.at[h, i, 0:n], g_recv.at[h, 0, i])
+        wait_bytes(from_right.at[h, i, 0:n], g_recv.at[h, 1, i])
+        total = mine + from_left[h, i, 0:n].astype(F32) + from_right[h, i, 0:n].astype(F32)
+        summed[h, i, 0:BLOCKS[h]] = total.astype(BF).reshape(BLOCKS[h], 32, 256)
+        near = CHUNK_ORDER_OUT[i] == 0
+        for step, dy in enumerate(Y_STEPS[h]):
+            to_y = lax.rem(y + 4 - dy, 4)
+            for dl in (1, 0):
+                to_lo = z_lo if dl == 0 else 1 - z_lo
+                src = summed.at[h, i, step * 2 + to_lo]
                 dst = final_in.at[row, z_hi]
-                if CHUNK_ORDER_OUT[i] == 0 and dl == 0 and dy == 0:
+                if near and dl == 0 and dy == 0:
                     local_copy(src, dst, z_recv)
                 else:
-                    send(src, dst, z_send.at[i], z_recv, place(to_lo, to_y, zc, x, core))
-
-    for way in range(2):
-        for i in range(4):
-            later(far_left.at[0], f_send.at[way, i])
-            later(from_left.at[0], g_send.at[way, i])
-    for i in range(4):
-        later(payload.at[0:7 if CHUNK_ORDER_OUT[i] == 0 else 8], z_send.at[i])
-    return_first(0)
-    return_first(1)
-    return_second(0)
-    return_first(2)
-    return_second(1)
-    return_third(0)
-    return_first(3)
-    return_second(2)
-    return_third(1)
-    return_second(3)
-    return_third(2)
-    return_third(3)
+                    send(src, dst, z_send.at[h, i], z_recv, place(to_lo, to_y, zc, x, core))
+        later(payload.at[0:BLOCKS[h] - (near and 0 in Y_STEPS[h])], z_send.at[h, i])
+
+    def wait_gate_up():
+        wait_bytes(gain, in_sem.at[3])
+        wait_bytes(gate_w.at[core], w_sem.at[1])
+        wait_bytes(up_w.at[core], w_sem.at[2])
+        wait_bytes(gate_w.at[other], wr_sem.at[1])
+        wait_bytes(up_w.at[other], wr_sem.at[2])
+
+    def wait_down():
+        wait_bytes(down_w.at[core], w_sem.at[3])
+        wait_bytes(down_w.at[other], wr_sem.at[3])
+
+    steps = dict(
+        d=dispatch, p=gather_first, q=gather_second, r=gather_third, e=exchange_first, f=exchange_second,
+        a=return_first, b=return_second, c=return_third,
+    )
+    for part in PLAN:
+        for name in part:
+            step, h = steps[name[0]], int(name[1])
+            if name[0] in "ef":
+                step(h)
+            else:
+                step(h, int(name[2]))
+        if part is PLAN[0]:
+            wait_gate_up()
+        if part is PLAN[1]:
+            wait_down()
 
     wait_bytes(final_in, z_recv)
     pieces = final_in[...].astype(F32).reshape(16, 2, 32, 256)
@@ -424,20 +462,21 @@
         pltpu.VMEM((2, 128, 512), BF),
         pltpu.VMEM((2, 128, 128), F32),
         pltpu.VMEM((16, 32, 256), BF),
-        pltpu.VMEM((4, 4, 8, 32, 256), BF),
-        pltpu.VMEM((4, 256, 256), F32),
-        pltpu.VMEM((4, 256, 256), F32),
-        pltpu.VMEM((256, 128), F32),
-        pltpu.VMEM((256, 128), F32),
-        pltpu.VMEM((2, 256, 256), BF),
-        pltpu.VMEM((4, 256, 256), BF),
-        pltpu.VMEM((4, 256, 256), BF),
-        pltpu.VMEM((4, 256, 256), BF),
-        pltpu.VMEM((4, 128, 256), BF),
-        pltpu.VMEM((4, 128, 256), BF),
-        pltpu.VMEM((4, 256, 256), BF),
-        pltpu.VMEM((4, 256, 256), BF),
-        pltpu.VMEM((4, 8, 32, 256), BF),
+        pltpu.VMEM((PARTS, 4, 4, MOST, 32, 256), BF),
+        pltpu.VMEM((PARTS, 4, MOST * 32, 256), F32),
+        pltpu.VMEM((PARTS, 4, MOST * 32, 256), F32),
+        pltpu.VMEM((PARTS, MOST * 32, 128), F32),
+        pltpu.VMEM((PARTS, MOST * 32, 128), F32),
+        pltpu.VMEM((PARTS, 2, MOST * 32, 256), BF),
+        pltpu.VMEM((PARTS, 4, MOST * 32, 256), BF),
+        pltpu.VMEM((PARTS, 4, MOST * 32, 256), BF),
+        pltpu.VMEM((PARTS, 4, MOST * 32, 256), BF),
+        pltpu.VMEM((PARTS, 4, 2, MOST * 16, 256), F32),
+        pltpu.VMEM((PARTS, 4, MOST * 16, 256), BF),
+        pltpu.VMEM((PARTS, 4, MOST * 16, 256), BF),
+        pltpu.VMEM((PARTS, 4, MOST * 32, 256), BF),
+        pltpu.VMEM((PARTS, 4, MOST * 32, 256), BF),
+        pltpu.VMEM((PARTS, 4, MOST, 32, 256), BF),
         pltpu.VMEM((8, 4, 32, 256), BF),
         dma((4,)),
         dma((4,)),
@@ -445,24 +484,24 @@
         dma((4,)),
         dma,
         dma((2,)),
-        dma((4,)),
-        dma((4,)),
+        dma((2, 3)),
+        dma((2, 3)),
         dma,
         dma((2,)),
-        dma((4,)),
-        dma((4,)),
-        dma((2, 4)),
-        dma((2, 4)),
-        dma((2, 4)),
-        dma((2, 4)),
-        dma((2,)),
-        dma((2,)),
-        dma((2, 4)),
-        dma((2, 4)),
-        dma((2, 4)),
-        dma((2, 4)),
+        dma((PARTS, 4)),
+        dma((PARTS, 4)),
+        dma((PARTS, 2, 4, 2)),
+        dma((PARTS, 2, 4, 2)),
+        dma((PARTS, 2, 4)),
+        dma((PARTS, 2, 4)),
+        dma((PARTS, 2)),
+        dma((PARTS, 2)),
+        dma((PARTS, 2, 4)),
+        dma((PARTS, 2, 4)),
+        dma((PARTS, 2, 4)),
+        dma((PARTS, 2, 4)),
         dma,
-        dma((4,)),
+        dma((PARTS, 4)),
     ]
     return pl.pallas_call(
         kernel,

time: 100 us -> 92.4 us (0.924)
  Pallas kernels: 98.5 us -> 90.2 us
    pallas_call x1, Pallas kernels: 98.5 us -> 90.2 us  [per_device(): pl.pallas_call(kernel, out_shape=jax.ShapeDtypeStruct((128, 256), BF), in...]
where the time goes in v3:
time: 92.4 us; the launch traced here: 91.7 us
  Pallas kernels  90.2 us (98%)
  local copies, waits for them, and re-layouts  1.47 us (2%)
    pallas_call x1, Pallas kernels, per_device(): pl.pallas_call(kernel, out_shape=jax.ShapeDtypeStruct((128, 256), BF), in...  90.2 us

profile of v3, /device:TPU:1, one launch (start us, length us, event | category | flops | bytes accessed | tf_op | source)
XLA Modules:
  0.0 91.7 jit_solution(13320117677795991373)
XLA Ops:
  0.0 90.2 %block.1 = bf16[128,256]{1,0:T(8,128)(2,1)} custom-call(bf16[128,256]{1,0:T(8,128)(2,1)} %stream.1, bf16[128,256]{1,0:T(8,128)(2,1)} %heads.1, bf16[1024,256]{1,0:T(8,128)(2,1)} %w_out.1, f32[32,1,256]{2,1,0:T(1,128)} %bitcast.7, s32[2,128]{1,0:T(2,128)} %bitcast.8, f32[2,128]{1,0:T(2,128)} %bitcast.9, bf16[16,2,256,256]{3,2,1,0:T(8,128)(2,1)} %bitcast.5, ...), custom_call_target="tpu_custom_call" | custom-call | tf_op jit(solution)/shard_map/block/pallas_call | solution.py:506
  90.2 1.5 %copy.11 = bf16[128,256]{1,0:T(8,128)(2,1)} copy(bf16[128,256]{1,0:T(8,128)(2,1)} %block.1) | data formatting | bytes 131072

commit v4 on v3

--- a/solution.py
+++ b/solution.py
@@ -11,7 +11,7 @@
 WIDTH = 8192
 CHUNK_ORDER_IN = (0, 1, 3, 2)
 CHUNK_ORDER_OUT = (2, 1, 3, 0)
-Y_STEPS = ((1, 3), (0, 2))
+Y_STEPS = ((0, 2), (1, 3))
 PARTS = len(Y_STEPS)
 BLOCKS = tuple(2 * len(part) for part in Y_STEPS)
 MOST = max(BLOCKS)
@@ -20,7 +20,7 @@
         "d00", "d01", "d03", "d02",
     ),
     (
-        "p00", "p01", "p02", "p03", "d10", "d11", "d13", "d12", "q00", "q01", "q02", "q03",
+        "p00", "p01", "p02", "d10", "p03", "d11", "d13", "d12", "q00", "q01", "q02", "q03",
         "r00", "r01", "r02", "r03", "e0", "p10", "p11", "p12", "p13", "q10", "q11", "q12",
         "q13", "f0",
     ),

time: 92.4 us -> 91.5 us (level)
  no operation moved by 1% of the time
where the time goes in v4:
time: 91.5 us; the launch traced here: 91.2 us
  Pallas kernels  89.7 us (98%)
  local copies, waits for them, and re-layouts  1.47 us (2%)
    pallas_call x1, Pallas kernels, per_device(): pl.pallas_call(kernel, out_shape=jax.ShapeDtypeStruct((128, 256), BF), in...  89.7 us

profile of v4, /device:TPU:1, one launch (start us, length us, event | category | flops | bytes accessed | tf_op | source)
XLA Modules:
  0.0 91.2 jit_solution(3263317323781598710)
XLA Ops:
  0.0 89.7 %block.1 = bf16[128,256]{1,0:T(8,128)(2,1)} custom-call(bf16[128,256]{1,0:T(8,128)(2,1)} %stream.1, bf16[128,256]{1,0:T(8,128)(2,1)} %heads.1, bf16[1024,256]{1,0:T(8,128)(2,1)} %w_out.1, f32[32,1,256]{2,1,0:T(1,128)} %bitcast.7, s32[2,128]{1,0:T(2,128)} %bitcast.8, f32[2,128]{1,0:T(2,128)} %bitcast.9, bf16[16,2,256,256]{3,2,1,0:T(8,128)(2,1)} %bitcast.5, ...), custom_call_target="tpu_custom_call" | custom-call | tf_op jit(solution)/shard_map/block/pallas_call | solution.py:506
  89.7 1.5 %copy.11 = bf16[128,256]{1,0:T(8,128)(2,1)} copy(bf16[128,256]{1,0:T(8,128)(2,1)} %block.1) | data formatting | bytes 131072

commit v5 on v4

--- a/solution.py
+++ b/solution.py
@@ -293,28 +293,25 @@
         zc = chunk_z(i)
         n = BLOCKS[h]
         wait_bytes(tokens.at[h, x, zc, 0:n], d1_recv.at[h, CHUNK_ORDER_IN[i]])
-        ends = (tokens.at[h, x, zc, 0:n // 2], tokens.at[h, x, zc, n // 2:n])
-        for k in range(2):
-            send(ends[k], ends[k], d2_send.at[h, 0, i, k], d2_recv.at[h, 0, i, k], right_dev)
-            send(ends[1 - k], ends[1 - k], d2_send.at[h, 1, i, k], d2_recv.at[h, 1, i, k], left_dev)
-            for way in range(2):
-                later(payload.at[0:n // 2], d2_send.at[h, way, i, k])
+        view = tokens.at[h, x, zc, 0:n]
+        send(view, view, d2_send.at[h, 0, i], d2_recv.at[h, 0, i], right_dev)
+        send(view, view, d2_send.at[h, 1, i], d2_recv.at[h, 1, i], left_dev)
+        for way in range(2):
+            later(payload.at[0:n], d2_send.at[h, way, i])
         absorb(h, x, zc)
 
     def gather_second(h, i):
         zc = chunk_z(i)
         n = BLOCKS[h]
+        wait_bytes(tokens.at[h, left, zc, 0:n], d2_recv.at[h, 0, i])
         view = tokens.at[h, left, zc, 0:n // 2]
-        wait_bytes(view, d2_recv.at[h, 0, i, 0])
         send(view, view, d3_send.at[h, 0, i], d3_recv.at[h, 0, i], right_dev)
+        wait_bytes(tokens.at[h, right, zc, 0:n], d2_recv.at[h, 1, i])
         view = tokens.at[h, right, zc, n // 2:n]
-        wait_bytes(view, d2_recv.at[h, 1, i, 0])
         send(view, view, d3_send.at[h, 1, i], d3_recv.at[h, 1, i], left_dev)
         for way in range(2):
             later(payload.at[0:n // 2], d3_send.at[h, way, i])
-        wait_bytes(tokens.at[h, left, zc, n // 2:n], d2_recv.at[h, 0, i, 1])
         absorb(h, left, zc)
-        wait_bytes(tokens.at[h, right, zc, 0:n // 2], d2_recv.at[h, 1, i, 1])
         absorb(h, right, zc)
 
     def gather_third(h, i):
@@ -490,8 +487,8 @@
         dma((2,)),
         dma((PARTS, 4)),
         dma((PARTS, 4)),
-        dma((PARTS, 2, 4, 2)),
-        dma((PARTS, 2, 4, 2)),
+        dma((PARTS, 2, 4)),
+        dma((PARTS, 2, 4)),
         dma((PARTS, 2, 4)),
         dma((PARTS, 2, 4)),
         dma((PARTS, 2)),

time: 91.5 us -> 92.3 us (level)
  no operation moved by 1% of the time
where the time goes in v5:
time: 92.3 us; the launch traced here: 91.5 us
  Pallas kernels  90 us (98%)
  local copies, waits for them, and re-layouts  1.47 us (2%)
    pallas_call x1, Pallas kernels, per_device(): pl.pallas_call(kernel, out_shape=jax.ShapeDtypeStruct((128, 256), BF), in...  90 us

profile of v5, /device:TPU:1, one launch (start us, length us, event | category | flops | bytes accessed | tf_op | source)
XLA Modules:
  0.0 91.5 jit_solution(16373745950083103429)
XLA Ops:
  0.0 90.0 %block.1 = bf16[128,256]{1,0:T(8,128)(2,1)} custom-call(bf16[128,256]{1,0:T(8,128)(2,1)} %stream.1, bf16[128,256]{1,0:T(8,128)(2,1)} %heads.1, bf16[1024,256]{1,0:T(8,128)(2,1)} %w_out.1, f32[32,1,256]{2,1,0:T(1,128)} %bitcast.7, s32[2,128]{1,0:T(2,128)} %bitcast.8, f32[2,128]{1,0:T(2,128)} %bitcast.9, bf16[16,2,256,256]{3,2,1,0:T(8,128)(2,1)} %bitcast.5, ...), custom_call_target="tpu_custom_call" | custom-call | tf_op jit(solution)/shard_map/block/pallas_call | solution.py:503
  90.0 1.5 %copy.11 = bf16[128,256]{1,0:T(8,128)(2,1)} copy(bf16[128,256]{1,0:T(8,128)(2,1)} %block.1) | data formatting | bytes 131072
